TPU v7x, 256 devices: a whole 4x4x8 slice. The times are simulated.
256 devices in a mesh: dev: 16 (over y, z_lo, core), ha: 16 (over x, z_hi).
Axes of the slice: x: 4, y: 4, z: 8 (z_hi: 4, z_lo: 2; z = z_hi * 2 + z_lo), core: 2. Of those that a mesh axis runs over, the one named last changes fastest.
Arguments:
- image: bfloat16 [32, 64, 256, 256], P(None, 'dev', 'ha'), may hold values from -6 to 6
- kernel_one: bfloat16 [64, 32, 3, 3, 3], replicated, may hold values from -0.21875 to 0.21875
- kernel_two: bfloat16 [128, 64, 3, 3, 3], P('ha'), may hold values from -0.15625 to 0.15625
- cotangent: bfloat16 [128, 16, 64, 64], P('ha', 'dev'), may hold values from -6 to 6
Outputs:
- activation: bfloat16 [128, 16, 64, 64], P('ha', 'dev')
- grad_pooled: bfloat16 [64, 16, 64, 64], P(None, 'dev', 'ha')
- grad_one: float32 [64, 32, 3, 3, 3], replicated
- grad_two: float32 [128, 64, 3, 3, 3], P('ha')
All inputs are finite; a program needn't handle non-finite values.
Results may differ from a plain program's by a relative error of at most 0.02.
Values may be sent and summed in bfloat16 or wider, within the bound.
No kernel may reach another device: no remote copies, remote signals or barrier semaphores. Data moves between devices by JAX's collectives and lax.ppermute only.
A program may use at most 128 MiB of HBM per device.

v0:
```python
import math

import jax
import jax.numpy as jnp
from jax import lax
from jax.sharding import PartitionSpec as P


def from_behind(block, axis, distance):
    devices = range(lax.axis_size(axis))
    route = [(i - distance, i) for i in devices if i - distance in devices]
    return lax.ppermute(block, axis, route)


def extended_2(shard, sides, width):
    for axis, dim in sides:
        size, length = (lax.axis_size(axis), shard.shape[dim])
        up = [(i, (i + 1) % size) for i in range(size - 1)]
        down = [(j, i) for i, j in up]
        last = lax.slice_in_dim(shard, length - width, length, axis=dim)
        initial = lax.slice_in_dim(shard, 0, width, axis=dim)
        before = lax.ppermute(last, axis, up)
        after = lax.ppermute(initial, axis, down)
        shard = jnp.concatenate([before, shard, after], axis=dim)
    return shard


def convolve(field, kernel, strides):
    return lax.conv_general_dilated(
        field[None],
        kernel,
        strides,
        "VALID",
        dimension_numbers=("NCDHW", "OIDHW", "NCDHW"),
        preferred_element_type=jnp.float32,
    )[0]


def filter_grad(field, deltas, dilation):
    result = lax.conv_general_dilated(
        field[None],
        deltas[None],
        (1, 1, 1),
        "VALID",
        rhs_dilation=(dilation, dilation, dilation),
        dimension_numbers=("CNDHW", "IODHW", "NCDHW"),
        preferred_element_type=jnp.float32,
    )
    return jnp.transpose(result, (1, 0, 2, 3, 4))


def average_pool(field):
    chans, depth, height, width = field.shape
    return field.reshape(chans, depth // 2, 2, height // 2, 2, width // 2, 2).mean(axis=(2, 4, 6))


def expand_pool(field):
    chans, depth, height, width = field.shape
    grown = jnp.broadcast_to(
        field[:, :, None, :, None, :, None], (chans, depth, 2, height, 2, width, 2)
    )
    return grown.reshape(chans, 2 * depth, 2 * height, 2 * width)


def silu_slope(value):
    sigma = jax.nn.sigmoid(value)
    return sigma * (1.0 + value * (1.0 - sigma))


def flip_kernel(kernel):
    return jnp.transpose(jnp.flip(kernel, (2, 3, 4)), (1, 0, 2, 3, 4))


def shards(image, kernel_one, kernel_two, cotangent):
    total_cells = (
        image.shape[1]
        * lax.axis_size("dev")
        * image.shape[2]
        * lax.axis_size("ha")
        * image.shape[3]
    )
    cells_one = total_cells // 8
    cells_two = total_cells // 64
    low_plane = from_behind(image[:, image.shape[1] - 1 :], "dev", 1)
    extended = jnp.concatenate([low_plane, image], axis=1)
    low_row = from_behind(extended[:, :, extended.shape[2] - 1 :], "ha", 1)
    extended = jnp.concatenate([low_row, extended], axis=2)
    extended = jnp.pad(extended, ((0, 0), (0, 0), (0, 0), (1, 0)))
    pre_one = convolve(extended, kernel_one, (2, 2, 2))
    pooled = average_pool(jax.nn.silu(pre_one)).astype(jnp.bfloat16)
    margin = extended_2(pooled, (("dev", 1),), 1)
    all_rows = lax.all_gather(margin, "ha", axis=2, tiled=True)
    rows_pad = jnp.pad(all_rows, ((0, 0), (0, 0), (1, 1), (1, 1)))
    pre_two = convolve(rows_pad, kernel_two, (1, 1, 1))
    activation = jax.nn.silu(pre_two).astype(jnp.bfloat16)
    delta_two = (cotangent.astype(jnp.float32) * silu_slope(pre_two)).astype(jnp.bfloat16)
    grad_two = lax.psum(filter_grad(rows_pad, delta_two, 1).astype(jnp.bfloat16), "dev").astype(
        jnp.float32
    ) / math.sqrt(cells_two)
    delta_margin = extended_2(delta_two, (("dev", 1),), 1)
    delta_pad = jnp.pad(delta_margin, ((0, 0), (0, 0), (1, 1), (1, 1)))
    partial_back = convolve(delta_pad, flip_kernel(kernel_two), (1, 1, 1))
    back_pooled = lax.psum_scatter(
        partial_back.astype(jnp.bfloat16), "ha", scatter_dimension=2, tiled=True
    ).astype(jnp.float32)
    grad_pooled = back_pooled.astype(jnp.bfloat16)
    delta_one = (expand_pool(back_pooled) * 0.125 * silu_slope(pre_one)).astype(jnp.bfloat16)
    grad_one = lax.psum(filter_grad(extended, delta_one, 2), ("dev", "ha")) * (
        8.0 / math.sqrt(cells_one)
    )
    return (activation, grad_pooled, grad_one, grad_two)


def solution(mesh):
    return jax.shard_map(
        shards,
        mesh=mesh,
        in_specs=(
            P(None, "dev", "ha", None),
            P(),
            P("ha", None, None, None, None),
            P("ha", "dev", None, None),
        ),
        out_specs=(
            P("ha", "dev", None, None),
            P(None, "dev", "ha", None),
            P(),
            P("ha", None, None, None, None),
        ),
        check_vma=False,
    )
```

profile of v0, /device:TPU:1, one launch (start us, length us, event | category | flops | bytes accessed | tf_op | source)
XLA Modules:
  0.0 617.4 jit_solution(11245860475050613281)
XLA Ops:
  8.3 4.9 collective-permute-start
  13.3 3.3 collective-permute-done
  18.4 4.9 collective-permute-start.1
  27.7 5.9 reshape.120
  33.6 10.7 %copy.88 = bf16[32,5,17,1,8,34]{0,4,5,2,1,3:T(8,128)(2,1)} copy(bf16[32,5,17,1,8,34]{5,4,0,2,1,3:T(8,128)(2,1)} %reshape.120) | data formatting | bytes 2959360 | tf_op jit(solution)/shard_map/conv_general_dilated | solution.py:29
  45.4 7.4 %add_multiply_fusion = (f32[2,8,8,17,64]{4,2,3,1,0:T(8,128)}, f32[2,8,8,17,64]{4,2,3,1,0:T(8,128)S(1)}) fusion(bf16[64,32,3,3,3]{0,1,4,3,2:T(8,128)(2,1)S(1)} %copy-done, bf16[32,5,17,1,7,2]{0,4,5,2,1,3:T(8,128)(2,1)S(1)} %slice.17, bf16[32,5,17,1,8,34]{0,4,5,2,1,3:T(8,128)(2,1)} %copy.88, pred[8,17]{0,1:T(8,128)(4,1)S(1)} %copy-done.9), kind=kOutput, calls=%fused_computation.38 | convolution fusion | flops 246601728 | bytes 2780680 | tf_op jit(solution)/shard_map/conv_general_dilated | solution.py:29
  53.8 5.2 collective-permute-start.2
  61.2 3.7 collective-permute-done.3
  67.2 71.3 %all-gather.2.cloned.1.call-done = bf16[64,3,64,64]{3,0,1,2:T(8,128)(2,1)} async-done(((bf16[64,3,4,64]{3,0,1,2:T(8,128)(2,1)}), bf16[64,3,64,64]{3,0,1,2:T(8,128)(2,1)}) %all-gather.2.cloned.1.call-update) | async-done | bytes 1572880 | tf_op jit(solution)/shard_map/all_gather | solution.py:92
  138.5 6.8 %copy.95 = bf16[64,3,64,64]{2,0,3,1:T(8,128)(2,1)} copy(bf16[64,3,64,64]{3,0,1,2:T(8,128)(2,1)} %all-gather.2.cloned.1.call-done) | data formatting | bytes 3145728 | tf_op jit(solution)/shard_map/all_gather | solution.py:92
  145.2 3.0 pad_bitcast_fusion.1
  150.9 6.4 %copy.97 = bf16[64,3,66,1,8,9]{0,4,5,2,1,3:T(8,128)(2,1)} copy(bf16[64,3,66,1,8,9]{2,0,5,4,1,3:T(8,128)(2,1)} %bitcast.70) | data formatting | bytes 3649536 | tf_op jit(solution)/shard_map/conv_general_dilated | solution.py:29
  158.8 11.6 %fusion.27 = f32[1,64,8,9,8]{4,2,3,1,0:T(8,128)} fusion(bf16[8,64,3,3,3]{1,0,4,3,2:T(8,128)(2,1)S(1)} %copy-done.8, bf16[64,3,66,1,7,2]{0,4,5,2,1,3:T(8,128)(2,1)S(1)} %slice.19, bf16[64,3,66,1,8,9]{0,4,5,2,1,3:T(8,128)(2,1)} %copy.97, pred[8,9]{0,1:T(8,128)(4,1)S(1)} %copy-done.10), kind=kOutput, calls=%fused_computation.31 | convolution fusion | flops 134129664 | bytes 2354760 | tf_op jit(solution)/shard_map/conv_general_dilated | solution.py:29
  170.4 3.0 copy.98
  177.2 3.6 collective-permute-start.5
  183.2 27.0 %copy.106 = bf16[1,32,5,17,257]{1,0,4,3,2:T(2,128)(2,1)} copy(bf16[1,32,5,17,257]{4,1,3,2,0:T(8,128)(2,1)} %get-tuple-element.22) | data formatting | bytes 2796160 | tf_op jit(solution)/shard_map/broadcast_in_dim | solution.py:30
  210.2 3.3 copy.110
  213.4 12.4 %copy.109 = bf16[1,64,3,66,66]{1,0,4,3,2:T(2,128)(2,1)} copy(bf16[1,64,3,66,66]{3,1,4,2,0:T(8,128)(2,1)S(1)} %get-tuple-element.20) | data formatting | bytes 3345408 | tf_op jit(solution)/shard_map/broadcast_in_dim | solution.py:30
  227.2 3.4 copy.101
  231.9 6.1 select_convert_fusion
  240.6 34.7 %convolution_convert_fusion = bf16[8,64,3,3,3]{1,0,4,3,2:T(8,128)(2,1)S(1)} fusion(bf16[1,64,3,66,66]{1,0,4,3,2:T(2,128)(2,1)} %copy.109, bf16[1,8,1,64,64]{1,0,4,3,2:T(2,128)(2,1)S(1)} %copy-done.3), kind=kOutput, calls=%fused_computation.37 | convolution fusion | flops 113260032 | bytes 1765888 | tf_op jit(solution)/shard_map/transpose | solution.py:49
  275.3 52.0 %psum.15 = bf16[8,64,3,3,3]{1,0,4,3,2:T(8,128)(2,1)} all-reduce(bf16[8,64,3,3,3]{1,0,4,3,2:T(8,128)(2,1)S(1)} %convolution_convert_fusion), channel_id=1, replica_groups=mesh['dev'=16,'ha'=16] {'dev'}, use_global_device_ids=true, to_apply=%region_4.5 | all-reduce | flops 13824 | bytes 55296 | tf_op jit(solution)/shard_map/psum | solution.py:97
  328.6 29.1 %fusion.38 = f32[64,32,3,3,3]{0,1,4,3,2:T(8,128)} fusion(bf16[1,32,5,17,257]{1,0,4,3,2:T(2,128)(2,1)} %copy.106, bf16[1,64,2,8,128]{1,3,4,2,0:T(8,128)(2,1)S(1)} %fusion.37), kind=kOutput, calls=%fused_computation.46 | convolution fusion | flops 226492416 | bytes 1881408 | tf_op jit(solution)/shard_map/transpose | solution.py:49
  359.9 248.9 %all-reduce.5.cloned.1.call-done = f32[64,32,3,3,3]{0,1,4,3,2:T(8,128)} async-done(((f32[64,32,3,3,3]{0,1,4,3,2:T(8,128)}), f32[64,32,3,3,3]{0,1,4,3,2:T(8,128)}) %all-reduce.5.cloned.1.call-update) | async-done | bytes 221200 | tf_op jit(solution)/shard_map/psum | solution.py:108
  (71 shorter events, 34.5 us)
Async XLA Ops:
  7.2 38.2 %copy-start = (bf16[64,32,3,3,3]{0,1,4,3,2:T(8,128)(2,1)S(1)}, bf16[64,32,3,3,3]{0,1,4,3,2:T(8,128)(2,1)}, u32[]{:S(2)}) copy-start(bf16[64,32,3,3,3]{0,1,4,3,2:T(8,128)(2,1)} %param.5) | copy-start | bytes 331780
  7.2 131.3 %all-gather.2.cloned.1.call-start = ((), (), s32[]{:S(2)}) async-start(), calls=%async_computation.1 | async-start | bytes 3342336 | tf_op jit(solution)/shard_map/all_gather | solution.py:92
  8.3 8.2 %collective-permute-start = (bf16[32,1,16,256]{3,0,2,1:T(8,128)(2,1)S(1)}, bf16[32,1,16,256]{3,0,2,1:T(8,128)(2,1)S(1)}, u32[]{:S(2)}, u32[]{:S(2)}) collective-permute-start(bf16[32,1,16,256]{3,0,2,1:T(8,128)(2,1)S(1)} %copy.118), channel_id=1, source_target_pairs={{0,16},{16,32},{32,48},{48,64},{64,80},{80,96},{96,112},{112,128},... | collective-permute-start | bytes 786440 | tf_op jit(solution)/shard_map/ppermute | solution.py:12
  18.4 6.4 %collective-permute-start.1 = (bf16[32,5,1,256]{3,0,2,1:T(8,128)(2,1)S(1)}, bf16[32,5,1,256]{3,0,2,1:T(8,128)(2,1)S(1)}, u32[]{:S(2)}, u32[]{:S(2)}) collective-permute-start(bf16[32,5,1,256]{3,0,2,1:T(8,128)(2,1)S(1)} %slice.16), channel_id=1, source_target_pairs={{0,1},{1,2},{2,3},{3,4},{4,5},{5,6},{6,7},{7,8},{8,9},{9,10},{10,1... | collective-permute-start | bytes 245768 | tf_op jit(solution)/shard_map/ppermute | solution.py:12
  33.6 11.8 %copy-start.9 = (pred[8,17]{0,1:T(8,128)(4,1)S(1)}, pred[8,17]{0,1:T(8,128)(4,1)}, u32[]{:S(2)}) copy-start(pred[8,17]{0,1:T(8,128)(4,1)} %constant.43) | copy-start | bytes 412
  52.8 13.6 %copy-start.7 = (bf16[8,1,64,64]{3,2,1,0:T(8,128)(2,1)S(1)}, bf16[8,1,64,64]{3,2,1,0:T(8,128)(2,1)}, u32[]{:S(2)}) copy-start(bf16[8,1,64,64]{3,2,1,0:T(8,128)(2,1)} %param.7) | copy-start | bytes 196612
  53.8 7.2 %collective-permute-start.2 = (bf16[64,1,4,64]{3,0,2,1:T(8,128)(2,1)S(1)}, bf16[64,1,4,64]{3,0,2,1:T(8,128)(2,1)S(1)}, u32[]{:S(2)}, u32[]{:S(2)}) collective-permute-start(bf16[64,1,4,64]{3,0,2,1:T(8,128)(2,1)S(1)} %copy.90), channel_id=1, source_target_pairs={{0,16},{16,32},{32,48},{48,64},{64,80},{80,96},{96,112},{112,128},... | collective-permute-start | bytes 98312 | tf_op jit(solution)/shard_map/ppermute | solution.py:22
  59.1 5.8 collective-permute-start.3
  66.0 261.3 %reduce-scatter.2.cloned.1.call-start = ((), (), s32[]{:S(2)}) async-start(), calls=%async_computation.2 | async-start | bytes 1114112 | tf_op jit(solution)/shard_map/reduce_scatter | solution.py:103
  150.9 7.8 %copy-start.8 = (bf16[8,64,3,3,3]{1,0,4,3,2:T(8,128)(2,1)S(1)}, bf16[8,64,3,3,3]{1,0,4,3,2:T(8,128)(2,1)}, u32[]{:S(2)}) copy-start(bf16[8,64,3,3,3]{1,0,4,3,2:T(8,128)(2,1)} %param.6) | copy-start | bytes 82948
  150.9 7.8 %copy-start.10 = (pred[8,9]{0,1:T(8,128)(4,1)S(1)}, pred[8,9]{0,1:T(8,128)(4,1)}, u32[]{:S(2)}) copy-start(pred[8,9]{0,1:T(8,128)(4,1)} %constant.42) | copy-start | bytes 220
  175.3 50.6 %collective-permute-start.4 = (bf16[8,1,64,64]{2,0,3,1:T(8,128)(2,1)S(1)}, bf16[8,1,64,64]{2,0,3,1:T(8,128)(2,1)}, u32[]{:S(2)}, u32[]{:S(2)}) collective-permute-start(bf16[8,1,64,64]{2,0,3,1:T(8,128)(2,1)S(1)} %get-tuple-element.26), channel_id=1, source_target_pairs={{0,16},{16,32},{32,48},{48,64},{64,80},{80,96},{96,112},{112,128},... | collective-permute-start | bytes 196616 | tf_op jit(solution)/shard_map/ppermute | solution.py:22
  177.2 48.7 %collective-permute-start.5 = (bf16[8,1,64,64]{2,0,3,1:T(8,128)(2,1)S(1)}, bf16[8,1,64,64]{2,0,3,1:T(8,128)(2,1)}, u32[]{:S(2)}, u32[]{:S(2)}) collective-permute-start(bf16[8,1,64,64]{2,0,3,1:T(8,128)(2,1)S(1)} %get-tuple-element.26), channel_id=1, source_target_pairs={{16,0},{32,16},{48,32},{64,48},{80,64},{96,80},{112,96},{128,112},... | collective-permute-start | bytes 196616 | tf_op jit(solution)/shard_map/ppermute | solution.py:23
  238.0 2.6 copy-start.3
  240.4 88.1 %copy-start.2 = (f32[2,8,8,17,64]{4,1,3,2,0:T(8,128)S(1)}, f32[2,8,8,17,64]{4,1,3,2,0:T(8,128)}, u32[]{:S(2)}) copy-start(f32[2,8,8,17,64]{4,1,3,2,0:T(8,128)} %copy.105) | copy-start | bytes 1671172
  240.4 368.4 %all-reduce.5.cloned.1.call-start = ((), (), s32[]{:S(2)}) async-start(), calls=%async_computation.3 | async-start | bytes 884736 | tf_op jit(solution)/shard_map/psum | solution.py:108
  328.6 29.2 %copy-start.6 = (bf16[8,64,3,3,3]{1,0,4,3,2:T(8,128)(2,1)S(1)}, bf16[8,64,3,3,3]{1,0,4,3,2:T(8,128)(2,1)}, u32[]{:S(2)}) copy-start(bf16[8,64,3,3,3]{1,0,4,3,2:T(8,128)(2,1)} %psum.15) | copy-start | bytes 82948
  328.6 29.8 %copy-start.4 = (bf16[8,1,64,64]{2,0,3,1:T(8,128)(2,1)S(1)}, bf16[8,1,64,64]{2,0,3,1:T(8,128)(2,1)}, u32[]{:S(2)}) copy-start(bf16[8,1,64,64]{2,0,3,1:T(8,128)(2,1)} %get-tuple-element.27) | copy-start | bytes 196612
  328.6 30.6 %copy-start.5 = (bf16[64,1,4,64]{3,0,1,2:T(8,128)(2,1)S(1)}, bf16[64,1,4,64]{3,0,1,2:T(8,128)(2,1)}, u32[]{:S(2)}) copy-start(bf16[64,1,4,64]{3,0,1,2:T(8,128)(2,1)} %reduce-scatter.2.cloned.1.call-done) | copy-start | bytes 98308
  328.6 282.0 %copy-start.1 = (bf16[64,32,3,3,3]{0,1,4,3,2:T(8,128)(2,1)S(1)}, bf16[64,32,3,3,3]{0,1,4,3,2:T(8,128)(2,1)}, u32[]{:S(2)}) copy-start(bf16[64,32,3,3,3]{0,1,4,3,2:T(8,128)(2,1)} %param.5) | copy-start | bytes 331780
Sparse Core Ops, SparseCore 0:
  66.2 72.2 all-gather.1
  240.5 84.0 reduce-scatter.1
  357.8 250.8 all-reduce.4
where the time goes:
time: 627 us; the launch traced here: 617 us
  waiting for transfers between devices  329 us (52%)
  local copies, waits for them, and re-layouts  100 us (16%)
  matrix products  88.9 us (14%)
  blocking collectives  52 us (8%)
  starting transfers between devices  23.1 us (4%)
  between operations  14.3 us (2%)
  other arithmetic  10 us (2%)
    psum x1, waiting for transfers between devices, shards(): lax.psum(filter_grad(extended, delta_one, 2), ('dev', 'ha'))  249 us
    all_gather x1, waiting for transfers between devices, shards(): all_rows = lax.all_gather(margin, 'ha', axis=2, tiled=True)  71.3 us
    transpose x2, matrix products, filter_grad(): return jnp.transpose(result, (1, 0, 2, 3, 4))  63.8 us
    psum x1, blocking collectives, shards(): lax.psum(filter_grad(rows_pad, delta_two, 1).astype(jnp.bfloat16), 'dev')  52 us
    broadcast_in_dim x6, local copies, waits for them, and re-layouts, convolve(): field[None]  45.4 us
    conv_general_dilated x8, local copies, waits for them, and re-layouts, convolve(): lax.conv_general_dilated(field[None], kernel, strides, 'VALID', dimension...  33.2 us
    conv_general_dilated x3, matrix products, convolve(): lax.conv_general_dilated(field[None], kernel, strides, 'VALID', dimension...  25.1 us
  transfers between devices with their start and end apart: 9, of which 5 were waited for; matrix products, arithmetic and copies ran while one was open for 13% of the time, Pallas kernels for 0%

commit v1 on v0

v1 whole, which is shorter than its diff:
```python
import math

import jax
import jax.numpy as jnp
from jax import lax
from jax.experimental import pallas as pl
from jax.experimental.pallas import tpu as pltpu
from jax.sharding import PartitionSpec as P

BF = jnp.bfloat16
F32 = jnp.float32
CELLS_ONE = 524288
CELLS_TWO = 65536
VMEM_LIMIT = 32 * 1024 * 1024


def call(body, out_shape, args, scratch=(), flops=1000000):
    moved = sum(math.prod(s.shape) * s.dtype.itemsize for s in list(out_shape) + list(args))
    return pl.pallas_call(
        body,
        out_shape=out_shape,
        in_specs=[pl.BlockSpec(memory_space=pltpu.VMEM)] * len(args),
        out_specs=[pl.BlockSpec(memory_space=pltpu.VMEM)] * len(out_shape),
        scratch_shapes=scratch,
        compiler_params=pltpu.CompilerParams(vmem_limit_bytes=VMEM_LIMIT),
        cost_estimate=pl.CostEstimate(flops=flops, bytes_accessed=moved, transcendentals=0),
    )(*args)


def shape(dims, dtype):
    return jax.ShapeDtypeStruct(dims, dtype)


def lanes(dims):
    return lax.broadcasted_iota(jnp.int32, dims, len(dims) - 1)


def rows_of(dims):
    return lax.broadcasted_iota(jnp.int32, dims, len(dims) - 2)


def mm(a, b):
    return lax.dot_general(a, b, (((1,), (0,)), ((), ())), preferred_element_type=F32)


def mm_nt(a, b):
    return lax.dot_general(a, b, (((1,), (1,)), ((), ())), preferred_element_type=F32)


def split_mm(a, sel, terms):
    total = None
    for _ in range(terms):
        part = a.astype(BF)
        a = a - part.astype(F32)
        term = mm(part, sel)
        total = term if total is None else total + term
    return total


def pack_filters_body(k_ref, cot_ref, out_ref, acc, cots):
    pieces = []
    for pair in range(14):
        left = k_ref[2 * pair].astype(F32)
        right = k_ref[2 * pair + 1].astype(F32) if pair < 13 else jnp.zeros((8, 64), F32)
        pieces.append(jnp.concatenate([left, right], axis=1))
    filters = jnp.concatenate(pieces, axis=1)
    for h in range(16):
        acc[8 * h : 8 * h + 8, 0:1792] = filters
    cots[...] = jnp.concatenate([cot_ref[...].astype(F32), jnp.zeros((512, 64), F32)], axis=1)
    for h in range(16):
        for half in range(2):
            row = 4 * h + 2 * half
            first = cots[pl.ds(row, 8, stride=64), :]
            second = cots[pl.ds(row + 1, 8, stride=64), :]
            acc[8 * h : 8 * h + 8, 1792 + 128 * half : 1920 + 128 * half] = first + pltpu.roll(second, 64, 1)
    out_ref[...] = acc[...].astype(BF)


def first_layer_body(x_ref, plane_ref, row_ref, corner_ref, w_ref, xt_ref, slope_ref, pooled_ref, top_ref, bot_ref, ev, od):
    w_in, n_out = rows_of((256, 256)), lanes((256, 256))
    sel = (w_in == jnp.where(n_out < 128, 2 * n_out, 2 * n_out - 255)).astype(F32).astype(BF)

    def spread(value, at):
        both = mm(value, sel)
        ev[at : at + value.shape[0], :] = both[:, :128]
        od[at : at + value.shape[0], :] = both[:, 128:]

    for part in range(8):
        spread(x_ref[256 * part : 256 * part + 256, :], 256 * part)
    for part in range(2):
        spread(plane_ref[256 * part : 256 * part + 256, :], 2048 + 256 * part)
    spread(row_ref[...], 2560)
    spread(corner_ref[...], 2688)

    first_lane = lanes((32, 128)) == 0
    for a in range(5):
        for b in range(17):
            if a > 0:
                start, stride = ((a - 1) * 16 + b - 1, 64) if b > 0 else (2560 + a - 1, 4)
            else:
                start, stride = (2048 + b - 1, 16) if b > 0 else (2688, 1)
            even = ev[pl.ds(start, 32, stride=stride), :]
            odd = od[pl.ds(start, 32, stride=stride), :]
            before = jnp.where(first_lane, 0.0, pltpu.roll(odd, 1, 1))
            xt_ref[a * 17 + b, 0:32, :] = before.astype(BF)
            xt_ref[a * 17 + b, 32:64, :] = even.astype(BF)
            xt_ref[a * 17 + b, 64:96, :] = odd.astype(BF)

    weights = jnp.transpose(w_ref[...].astype(F32), (1, 0)).astype(BF)
    sums = [None] * 4
    for i in range(2):
        for jp in range(4):
            pre = mm(weights, patches_one(xt_ref, i, jp))
            sigma = jax.nn.sigmoid(pre)
            at = (i * 4 + jp) * 256
            slope_ref[:, at : at + 256] = sigma * (1.0 + pre * (1.0 - sigma)) * 0.125
            act = pre * sigma
            both = act[:, :128] + act[:, 128:]
            sums[jp] = both if i == 0 else sums[jp] + both
    k_in, k_out = rows_of((256, 128)), lanes((256, 128))
    fold = ((k_in // 2) == k_out).astype(F32).astype(BF)
    halves = []
    for pair in range(2):
        stacked = jnp.concatenate([sums[2 * pair], sums[2 * pair + 1]], axis=1)
        halves.append(split_mm(stacked, fold, 3) * 0.125)
    pooled = jnp.concatenate(halves, axis=1)
    pooled_ref[...] = pooled.astype(BF)
    top_ref[...] = pooled[:, 0:64].astype(BF)
    bot_ref[...] = pltpu.roll(pooled, 64, 1)[:, 0:64].astype(BF)


def patches_one(xt_ref, i, jp):
    columns = []
    for j in (2 * jp, 2 * jp + 1):
        blocks = [xt_ref[(2 * i + a) * 17 + 2 * j + b] for a in range(3) for b in range(3)]
        columns.append(jnp.concatenate(blocks, axis=0))
    return jnp.concatenate(columns, axis=1)


def shifted(ext):
    dims = ext.shape
    column = lanes(dims) & 63
    for e in range(3):
        if e == 0:
            moved = jnp.where(column == 0, 0.0, pltpu.roll(ext, 1, 1))
        elif e == 2:
            moved = jnp.where(column == 63, 0.0, pltpu.roll(ext, 383, 1))
        else:
            moved = ext
        yield (0, e), moved[:, 0:256]
        yield (1, e), pltpu.roll(moved, 320, 1)[:, 0:256]
        yield (2, e), moved[:, 128:384]


def second_layer_body(before_ref, own_ref, after_ref, a2_ref, patches_ref, act_ref, delta_ref, top_ref, bot_ref):
    for a, ref in enumerate((before_ref, own_ref, after_ref)):
        for (b, e), value in shifted(ref[...].astype(F32)):
            t = a * 9 + b * 3 + e
            patches_ref[64 * t : 64 * t + 64, :] = value.astype(BF)
    patches_ref[1728:1792, :] = jnp.zeros((64, 256), BF)
    pre = mm(a2_ref[:, 0:1792], patches_ref[...])
    sigma = jax.nn.sigmoid(pre)
    act_ref[...] = (pre * sigma).astype(BF)
    slope = sigma * (1.0 + pre * (1.0 - sigma))
    delta = a2_ref[:, 1792:2048].astype(F32) * slope
    delta_ref[...] = delta.astype(BF)
    top_ref[...] = delta[:, 0:64].astype(BF)
    bot_ref[...] = pltpu.roll(delta, 64, 1)[:, 0:64].astype(BF)


def grad_two_body(delta_ref, patches_ref, out_ref):
    r, o = rows_of((128, 128)), lanes((128, 128))
    order = (o == (r % 16) * 8 + r // 16).astype(F32).astype(BF)
    delta = mm(order, delta_ref[...]).astype(BF)
    grad = mm_nt(delta, patches_ref[...]).astype(BF)
    for q in range(8):
        for half in range(2):
            d = 2 * q + half
            out_ref[16 * d : 16 * d + 16, :] = grad[16 * q : 16 * q + 16, 896 * half : 896 * half + 896]


def turn_filters_body(a2_ref, out_ref):
    for pair in range(14):
        block = a2_ref[:, 128 * pair : 128 * pair + 128].astype(F32)
        turned = jnp.transpose(block, (1, 0)).astype(BF)
        out_ref[:, 256 * pair : 256 * pair + 128] = turned[0:64, :]
        if pair < 13:
            out_ref[:, 256 * pair + 128 : 256 * pair + 256] = turned[64:128, :]


def backward_body(before_ref, own_ref, after_ref, wb_ref, slope_ref, xt_ref, g2_ref, pooled_ref, out_ref, pd, one):
    for a, ref in enumerate((before_ref, own_ref, after_ref)):
        for (b, e), value in shifted(ref[...].astype(F32)):
            t = 26 - (a * 9 + b * 3 + e)
            pd[128 * t : 128 * t + 128, :] = value.astype(BF)
    back = mm(wb_ref[...], pd[...])
    for r in range(4):
        turned = back if r == 0 else pltpu.roll(back, 256 - 64 * r, 1)
        pooled_ref[:, r, :] = turned[:, 0:64].astype(BF)
    w_in, n_out = rows_of((128, 256)), lanes((128, 256))
    total = jnp.zeros((64, 1024), F32)
    grown = []
    for pair in range(2):
        grow = (w_in == n_out // 2).astype(F32).astype(BF)
        grown.append(split_mm(back[:, 128 * pair : 128 * pair + 128], grow, 3))
    for i in range(2):
        for jp in range(4):
            row = grown[jp // 2][:, 128 * (jp % 2) : 128 * (jp % 2) + 128]
            at = (i * 4 + jp) * 256
            delta = (jnp.concatenate([row, row], axis=1) * slope_ref[:, at : at + 256]).astype(BF)
            cells = patches_one(xt_ref, i, jp)
            blank = jnp.zeros((32, 256), BF)
            chunks = []
            for s in range(4):
                chunks += [cells[224 * s : min(224 * s + 224, 864), :], blank]
            chunks.append(blank)
            total = total + mm_nt(delta, jnp.concatenate(chunks, axis=0))
    for s in range(4):
        for quarter in range(4):
            for side in range(2):
                at = 256 * s + 128 * side
                one[side, pl.ds(s * 4 + quarter, 16, stride=16), :] = total[16 * quarter : 16 * quarter + 16, at : at + 128]
    out_ref[:, 0:896] = g2_ref[...]
    out_ref[:, 896:1024] = one[0].astype(BF)
    out_ref[:, 1024:1152] = one[1].astype(BF)


def sum_depth_body(in_ref, act_ref, out_ref, acc):
    total = in_ref[0:16, :].astype(F32)
    for d in range(1, 16):
        total = total + in_ref[16 * d : 16 * d + 16, :].astype(F32)
    act = act_ref[...].astype(F32)
    acc[...] = jnp.zeros(acc.shape, F32)
    for side in range(2):
        for m in range(4):
            at = 256 * m + 128 * side
            if at < 896:
                acc[side, pl.ds(8 + m, 16, stride=16), :] = total[:, at : at + 128]
        for h in range(16):
            acc[side, 16 * h : 16 * h + 8, :] = act[8 * h : 8 * h + 8, 128 * side : 128 * side + 128]
        out_ref[:, 256 + 128 * side : 384 + 128 * side] = acc[side].astype(BF)
    one = total[:, 896:1152].astype(BF)
    for h in range(16):
        out_ref[16 * h : 16 * h + 16, 0:256] = one


def sum_height_body(in_ref, act_ref, out_ref, acc):
    total = in_ref[0:16, :].astype(F32)
    for h in range(16):
        block = in_ref[16 * h : 16 * h + 16, :].astype(F32)
        if h > 0:
            total = total + block
        for r in range(4):
            side, odd = r // 2, r % 2
            value = block[0:8, 256 + 128 * side : 384 + 128 * side]
            acc[pl.ds(4 * h + r, 8, stride=64), :] = pltpu.roll(value, 64, 1) if odd else value
    act_ref[...] = acc[...][:, 0:64].astype(BF)
    for d in range(16):
        out_ref[24 * d : 24 * d + 16, :] = total[:, 0:256]
        out_ref[24 * d + 16 : 24 * d + 24, :] = total[8:16, 256:512]


def finish_body(in_ref, one_ref, two_ref, acc):
    for side in range(2):
        acc[side, :, :] = in_ref[:, 128 * side : 128 * side + 128]
    for half in range(2):
        for m in range(4):
            for side in range(2):
                if 256 * m + 128 * side >= 896:
                    continue
                value = acc[side, pl.ds(24 * half + 16 + m, 8, stride=48), :] * (1.0 / math.sqrt(CELLS_TWO))
                t = 14 * half + 4 * m + 2 * side
                two_ref[t] = value[:, 0:64]
                if t + 1 < 27:
                    two_ref[t + 1] = pltpu.roll(value, 64, 1)[:, 0:64]
    scale = 8.0 / math.sqrt(CELLS_ONE)
    for s in range(4):
        for side in range(2):
            rows = [acc[side, pl.ds(s * 4 + quarter, 16, stride=24), :] for quarter in range(4)]
            turned = jnp.transpose(jnp.concatenate(rows, axis=0), (1, 0)) * scale
            for k in range(4):
                t = 7 * s + 4 * side + k
                if 4 * side + k < 7 and t < 27:
                    one_ref[t] = turned[32 * k : 32 * k + 32, :]


def move(block, axis, step):
    size = lax.axis_size(axis)
    return lax.ppermute(block, axis, [(i, i + step) for i in range(size) if 0 <= i + step < size])


def exchange(block, axis):
    return lax.all_to_all(block, axis, 0, 0, tiled=True)


def with_rims(own, top, bot):
    wide = jnp.concatenate([move(bot, "ha", 1), own, move(top, "ha", -1)], axis=1)
    return move(wide, "dev", 1), wide, move(wide, "dev", -1)


def shards(image, kernel_one, kernel_two, cotangent):
    n_dev, n_ha = lax.axis_size("dev"), lax.axis_size("ha")
    x = image.reshape(2048, 256)
    plane = move(image[:, 3].reshape(512, 256), "dev", 1)
    row = move(image[:, :, 15].reshape(128, 256), "ha", 1)
    corner = lax.ppermute(
        image[:, 3, 15],
        ("dev", "ha"),
        [(d * n_ha + h, (d + 1) * n_ha + h + 1) for d in range(n_dev - 1) for h in range(n_ha - 1)],
    )
    k1 = jnp.transpose(kernel_one, (2, 3, 4, 1, 0)).reshape(864, 64)
    k2 = jnp.transpose(kernel_two, (2, 3, 4, 0, 1)).reshape(27, 8, 64)
    cot = cotangent.reshape(512, 64)
    (packed,) = call(
        pack_filters_body,
        [shape((128, 2048), BF)],
        [k2, cot],
        [pltpu.VMEM((128, 2048), F32), pltpu.VMEM((512, 128), F32)],
    )
    a2 = exchange(packed, "ha")
    xt, slope, pooled, top, bot = call(
        first_layer_body,
        [shape((85, 96, 128), BF), shape((64, 2048), F32), shape((64, 256), BF), shape((64, 64), BF), shape((64, 64), BF)],
        [x, plane, row, corner, k1],
        [pltpu.VMEM((2720, 128), F32), pltpu.VMEM((2720, 128), F32)],
        flops=500000000,
    )
    (wb,) = call(turn_filters_body, [shape((64, 3456), BF)], [a2])
    before, own, after = with_rims(pooled, top, bot)
    patches, act, delta, dtop, dbot = call(
        second_layer_body,
        [shape((1792, 256), BF), shape((128, 256), BF), shape((128, 256), BF), shape((128, 64), BF), shape((128, 64), BF)],
        [before, own, after, a2],
        flops=120000000,
    )
    (g2,) = call(grad_two_body, [shape((256, 896), BF)], [delta, patches], flops=120000000)
    dbefore, down, dafter = with_rims(delta, dtop, dbot)
    grad_pooled, payload = call(
        backward_body,
        [shape((64, 4, 64), BF), shape((256, 1152), BF)],
        [dbefore, down, dafter, wb, slope, xt, g2],
        [pltpu.VMEM((3456, 256), BF), pltpu.VMEM((2, 256, 128), F32)],
        flops=400000000,
    )
    (second,) = call(
        sum_depth_body, [shape((256, 512), BF)], [exchange(payload, "dev"), act], [pltpu.VMEM((2, 256, 128), F32)]
    )
    activation, third = call(
        sum_height_body,
        [shape((512, 64), BF), shape((384, 256), F32)],
        [exchange(second, "ha")],
        [pltpu.VMEM((512, 128), F32)],
    )
    one, two = call(
        finish_body,
        [shape((27, 32, 64), F32), shape((27, 8, 64), F32)],
        [exchange(third, "dev")],
        [pltpu.VMEM((2, 384, 128), F32)],
    )
    grad_one = jnp.transpose(one.reshape(3, 3, 3, 32, 64), (4, 3, 0, 1, 2))
    grad_two = jnp.transpose(two.reshape(3, 3, 3, 8, 64), (3, 4, 0, 1, 2))
    return (activation.reshape(8, 1, 64, 64), grad_pooled.reshape(64, 1, 4, 64), grad_one, grad_two)


def solution(mesh):
    return jax.shard_map(
        shards,
        mesh=mesh,
        in_specs=(
            P(None, "dev", "ha", None),
            P(),
            P("ha", None, None, None, None),
            P("ha", "dev", None, None),
        ),
        out_specs=(
            P("ha", "dev", None, None),
            P(None, "dev", "ha", None),
            P(),
            P("ha", None, None, None, None),
        ),
        check_vma=False,
    )
```

time: 627 us -> 136 us (0.22); the launches traced: 617 us -> 136 us
  waiting for transfers between devices: 329 us -> 14.6 us
  local copies, waits for them, and re-layouts: 100 us -> 7.29 us
  matrix products: 88.9 us -> 0 us
  starting transfers between devices: 23.1 us -> 50.7 us
  between operations: 14.3 us -> 0.84 us
  Pallas kernels: 0 us -> 9.88 us
  other arithmetic: 10 us -> 0.19 us
    psum x1 -> x0, waiting for transfers between devices: 249 us -> none  [shards(): lax.psum(filter_grad(extended, delta_one, 2), ('dev', 'ha'))]
    all_gather x1 -> x0, waiting for transfers between devices: 71.3 us -> none  [shards(): all_rows = lax.all_gather(margin, 'ha', axis=2, tiled=True)]
    transpose x2 -> x0, matrix products: 63.8 us -> none  [filter_grad(): return jnp.transpose(result, (1, 0, 2, 3, 4))]
    all_to_all x0 -> x3, blocking collectives: none -> 52.1 us  [exchange(): return lax.all_to_all(block, axis, 0, 0, tiled=True)]
    psum x1 -> x0, blocking collectives: 52 us -> none  [shards(): lax.psum(filter_grad(rows_pad, delta_two, 1).astype(jnp.bfloat16), 'dev')]
    broadcast_in_dim x8 -> x0, local copies, waits for them, and re-layouts: 48.8 us -> none  [the longest x6 45.4 us: convolve(): field[None]]
    conv_general_dilated x8 -> x0, local copies, waits for them, and re-layouts: 33.2 us -> none  [convolve(): lax.conv_general_dilated(field[None], kernel, strides, 'VALID', dimension...]
    conv_general_dilated x3 -> x0, matrix products: 25.1 us -> none  [convolve(): lax.conv_general_dilated(field[None], kernel, strides, 'VALID', dimension...]
  transfers between devices with their start and end apart: 9 -> 12, of which waited for: 5 -> 5; matrix products, arithmetic and copies ran while one was open for 13% -> 3% of each run, Pallas kernels for 0% -> 3%
where the time goes in v1:
time: 136 us
  blocking collectives  52.1 us (38%)
  starting transfers between devices  50.7 us (37%)
  waiting for transfers between devices  14.6 us (11%)
  Pallas kernels  9.88 us (7%)
  local copies, waits for them, and re-layouts  7.29 us (5%)
    all_to_all x3, blocking collectives, exchange(): return lax.all_to_all(block, axis, 0, 0, tiled=True)  52.1 us
    ppermute x10, starting transfers between devices, move(): lax.ppermute(block, axis, [(i, i + step) for i in range(size) if 0 <= i +...  33.9 us
    ppermute x10, waiting for transfers between devices, move(): lax.ppermute(block, axis, [(i, i + step) for i in range(size) if 0 <= i +...  13.6 us
    all_to_all x1, starting transfers between devices, exchange(): return lax.all_to_all(block, axis, 0, 0, tiled=True)  11.6 us
    pallas_call x9, Pallas kernels, call(): pl.pallas_call(body, out_shape=out_shape, in_specs=[pl.BlockSpec(memory_s...  9.88 us
    ppermute x1, starting transfers between devices, shards(): lax.ppermute(image[:, 3, 15], ('dev', 'ha'), [(d * n_ha + h, (d + 1) * n_...  5.21 us
    unnamed x9, local copies, waits for them, and re-layouts  3.88 us
  transfers between devices with their start and end apart: 12, of which 5 were waited for; matrix products, arithmetic and copies ran while one was open for 3% of the time, Pallas kernels for 3%

profile of v1, /device:TPU:1, one launch (start us, length us, event | category | flops | bytes accessed | tf_op | source)
XLA Modules:
  0.0 135.6 jit_solution(4196362078999270303)
XLA Ops:
  2.4 1.0 shard_map.76
  3.4 11.6 %all-to-all-start = ((bf16[16,8,2048]{2,1,0:T(8,128)(2,1)}), bf16[16,8,2048]{2,1,0:T(8,128)(2,1)S(1)}, u32[]{:S(2)}, u32[]{:S(2)}) async-start(bf16[16,8,2048]{2,1,0:T(8,128)(2,1)} %bitcast.8), calls=%async_computation | async-start | bytes 1048576 | tf_op jit(solution)/shard_map/all_to_all | solution.py:293
  15.9 3.5 %collective-permute-start = (bf16[512,256]{1,0:T(8,128)(2,1)S(1)}, bf16[512,256]{1,0:T(8,128)(2,1)S(1)}, u32[]{:S(2)}, u32[]{:S(2)}) collective-permute-start(bf16[512,256]{1,0:T(8,128)(2,1)S(1)} %bitcast.44), channel_id=1, source_target_pairs={{0,16},{16,32},{32,48},{48,64},{64,80},{80,96},{96,112},{112,128},... | collective-permute-start | bytes 786440 | tf_op jit(solution)/shard_map/ppermute | solution.py:289
  19.4 1.5 %slice_reduce_fusion = bf16[32,4,256]{2,1,0:T(4,128)(2,1)S(1)} fusion(bf16[32,4,16,256]{3,2,1,0:T(8,128)(2,1)} %param.4), kind=kLoop, calls=%fused_computation | loop fusion | bytes 131072 | tf_op jit(solution)/shard_map/slice | solution.py:305
  20.9 4.4 %collective-permute-start.1 = (bf16[128,256]{1,0:T(8,128)(2,1)S(1)}, bf16[128,256]{1,0:T(8,128)(2,1)S(1)}, u32[]{:S(2)}, u32[]{:S(2)}) collective-permute-start(bf16[128,256]{1,0:T(8,128)(2,1)S(1)} %reshape_squeeze.7), channel_id=1, source_target_pairs={{0,1},{1,2},{2,3},{3,4},{4,5},{5,6},{6,7},{7,8},{8,9},{9,10},{10,1... | collective-permute-start | bytes 196616 | tf_op jit(solution)/shard_map/ppermute | solution.py:289
  26.3 5.2 %collective-permute-start.2 = (bf16[32,256]{1,0:T(8,128)(2,1)S(1)}, bf16[32,256]{1,0:T(8,128)(2,1)S(1)}, u32[]{:S(2)}, u32[]{:S(2)}) collective-permute-start(bf16[32,256]{1,0:T(8,128)(2,1)S(1)} %bitcast.45), channel_id=1, source_target_pairs={{0,17},{1,18},{2,19},{3,20},{4,21},{5,22},{6,23},{7,24},{8,25},{9,... | collective-permute-start | bytes 49160 | tf_op jit(solution)/shard_map/ppermute | solution.py:306
  32.5 1.2 copy-done
  34.7 2.7 %shard_map.75 = (bf16[85,96,128]{2,1,0:T(8,128)(2,1)S(1)}, f32[64,2048]{1,0:T(8,128)S(1)}, bf16[64,256]{1,0:T(8,128)(2,1)S(1)}, bf16[64,64]{1,0:T(8,128)(2,1)S(1)}, bf16[64,64]{1,0:T(8,128)(2,1)S(1)}) custom-call(bf16[2048,256]{1,0:T(8,128)(2,1)S(1)} %bitcast.40, bf16[512,256]{1,0:T(8,128)(2,1)S(1)} %collective-permute-done.plane_ref, ...), custom_call_target="tpu_custom_call" | custom-call | flops 500000000 | bytes 4165632 | tf_op jit(solution)/shard_map/pallas_call | solution.py:19
  37.4 5.3 %collective-permute-start.3 = (bf16[64,64]{1,0:T(8,128)(2,1)S(1)}, bf16[64,64]{1,0:T(8,128)(2,1)S(1)}, u32[]{:S(2)}, u32[]{:S(2)}) collective-permute-start(bf16[64,64]{1,0:T(8,128)(2,1)S(1)} %get-tuple-element.20), channel_id=1, source_target_pairs={{0,1},{1,2},{2,3},{3,4},{4,5},{5,6},{6,7},{7,8},{8,9},{9,10},{10,1... | collective-permute-start | bytes 24584 | tf_op jit(solution)/shard_map/ppermute | solution.py:289
  42.7 1.3 collective-permute-start.4
  44.0 4.3 %collective-permute-done.4 = bf16[64,64]{1,0:T(8,128)(2,1)S(1)} collective-permute-done((bf16[64,64]{1,0:T(8,128)(2,1)S(1)}, bf16[64,64]{1,0:T(8,128)(2,1)S(1)}, u32[]{:S(2)}, u32[]{:S(2)}) %collective-permute-start.4) | collective-permute-done | bytes 8224 | tf_op jit(solution)/shard_map/ppermute | solution.py:289
  48.4 4.9 %collective-permute-start.5 = (bf16[64,384]{1,0:T(8,128)(2,1)S(1)}, bf16[64,384]{1,0:T(8,128)(2,1)S(1)}, u32[]{:S(2)}, u32[]{:S(2)}) collective-permute-start(bf16[64,384]{1,0:T(8,128)(2,1)S(1)} %pad_maximum_fusion.1.own_ref), channel_id=1, source_target_pairs={{0,16},{16,32},{32,48},{48,64},{64,80},{80,96},{96,112},{112,128},... | collective-permute-start | bytes 147464 | tf_op jit(solution)/shard_map/ppermute | solution.py:289
  53.3 1.9 %collective-permute-start.6 = (bf16[64,384]{1,0:T(8,128)(2,1)S(1)}, bf16[64,384]{1,0:T(8,128)(2,1)S(1)}, u32[]{:S(2)}, u32[]{:S(2)}) collective-permute-start(bf16[64,384]{1,0:T(8,128)(2,1)S(1)} %pad_maximum_fusion.1.own_ref), channel_id=1, source_target_pairs={{16,0},{32,16},{48,32},{64,48},{80,64},{96,80},{112,96},{128,112},... | collective-permute-start | bytes 147464 | tf_op jit(solution)/shard_map/ppermute | solution.py:289
  55.3 3.5 %collective-permute-done.6.after_ref = bf16[64,384]{1,0:T(8,128)(2,1)S(1)} collective-permute-done((bf16[64,384]{1,0:T(8,128)(2,1)S(1)}, bf16[64,384]{1,0:T(8,128)(2,1)S(1)}, u32[]{:S(2)}, u32[]{:S(2)}) %collective-permute-start.6) | collective-permute-done | bytes 49184 | tf_op jit(solution)/shard_map/ppermute | solution.py:289
  59.4 5.7 %collective-permute-start.7 = (bf16[128,64]{1,0:T(8,128)(2,1)S(1)}, bf16[128,64]{1,0:T(8,128)(2,1)S(1)}, u32[]{:S(2)}, u32[]{:S(2)}) collective-permute-start(bf16[128,64]{1,0:T(8,128)(2,1)S(1)} %get-tuple-element.23), channel_id=1, source_target_pairs={{0,1},{1,2},{2,3},{3,4},{4,5},{5,6},{6,7},{7,8},{8,9},{9,10},{10,1... | collective-permute-start | bytes 49160 | tf_op jit(solution)/shard_map/ppermute | solution.py:289
  65.1 1.3 collective-permute-start.8
  66.5 4.9 %collective-permute-done.8 = bf16[128,64]{1,0:T(8,128)(2,1)S(1)} collective-permute-done((bf16[128,64]{1,0:T(8,128)(2,1)S(1)}, bf16[128,64]{1,0:T(8,128)(2,1)S(1)}, u32[]{:S(2)}, u32[]{:S(2)}) %collective-permute-start.8) | collective-permute-done | bytes 16416 | tf_op jit(solution)/shard_map/ppermute | solution.py:289
  71.5 1.9 %collective-permute-start.10 = (bf16[128,384]{1,0:T(8,128)(2,1)S(1)}, bf16[128,384]{1,0:T(8,128)(2,1)S(1)}, u32[]{:S(2)}, u32[]{:S(2)}) collective-permute-start(bf16[128,384]{1,0:T(8,128)(2,1)S(1)} %pad_maximum_fusion.own_ref), channel_id=1, source_target_pairs={{16,0},{32,16},{48,32},{64,48},{80,64},{96,80},{112,96},{128,112},... | collective-permute-start | bytes 294920 | tf_op jit(solution)/shard_map/ppermute | solution.py:289
  73.4 3.6 %collective-permute-start.9 = (bf16[128,384]{1,0:T(8,128)(2,1)S(1)}, bf16[128,384]{1,0:T(8,128)(2,1)S(1)}, u32[]{:S(2)}, u32[]{:S(2)}) collective-permute-start(bf16[128,384]{1,0:T(8,128)(2,1)S(1)} %pad_maximum_fusion.own_ref), channel_id=1, source_target_pairs={{0,16},{16,32},{32,48},{48,64},{64,80},{80,96},{96,112},{112,128},... | collective-permute-start | bytes 294920 | tf_op jit(solution)/shard_map/ppermute | solution.py:289
  78.7 2.8 %shard_map.80 = (bf16[64,4,64]{2,1,0:T(4,128)(2,1)}, bf16[256,1152]{1,0:T(8,128)(2,1)S(1)}) custom-call(bf16[128,384]{1,0:T(8,128)(2,1)S(1)} %collective-permute-done.9.before_ref, bf16[128,384]{1,0:T(8,128)(2,1)S(1)} %pad_maximum_fusion.own_ref, bf16[128,384]{1,0:T(8,128)(2,1)S(1)} %collective-permute-done.10.after_ref, ...), custom_call_target="tpu_custom_call" | custom-call | flops 400000000 | bytes 4431872 | tf_op jit(solution)/shard_map/pallas_call | solution.py:19
  81.5 17.1 %all_to_all.44 = bf16[16,16,1152]{2,1,0:T(8,128)(2,1)S(1)} all-to-all(bf16[16,16,1152]{2,1,0:T(8,128)(2,1)S(1)} %bitcast.38), channel_id=1, replica_groups=mesh['dev'=16,'ha'=16] {'dev'}, dimensions={0} | all-to-all | bytes 1179648 | tf_op jit(solution)/shard_map/all_to_all | solution.py:293
  98.7 22.7 %all_to_all.45 = bf16[16,16,512]{2,1,0:T(8,128)(2,1)S(1)} all-to-all(bf16[16,16,512]{2,1,0:T(8,128)(2,1)S(1)} %bitcast.36), channel_id=1, replica_groups=mesh['dev'=16,'ha'=16] {'ha'}, dimensions={0} | all-to-all | bytes 524288 | tf_op jit(solution)/shard_map/all_to_all | solution.py:293
  122.4 12.2 %all_to_all.46 = f32[16,24,256]{2,1,0:T(8,128)S(1)} all-to-all(f32[16,24,256]{2,1,0:T(8,128)S(1)} %bitcast.39), channel_id=1, replica_groups=mesh['dev'=16,'ha'=16] {'dev'}, dimensions={0} | all-to-all | bytes 786432 | tf_op jit(solution)/shard_map/all_to_all | solution.py:293
  134.6 1.0 shard_map.83
  (27 shorter events, 9.0 us)
Async XLA Ops:
  0.6 0.9 copy-start.1
  1.5 0.8 copy-start.2
  3.4 55.4 %all-to-all-start = ((bf16[16,8,2048]{2,1,0:T(8,128)(2,1)}), bf16[16,8,2048]{2,1,0:T(8,128)(2,1)S(1)}, u32[]{:S(2)}, u32[]{:S(2)}) async-start(bf16[16,8,2048]{2,1,0:T(8,128)(2,1)} %bitcast.8), calls=%async_computation | async-start | bytes 1048576 | tf_op jit(solution)/shard_map/all_to_all | solution.py:293
  15.9 16.6 %collective-permute-start = (bf16[512,256]{1,0:T(8,128)(2,1)S(1)}, bf16[512,256]{1,0:T(8,128)(2,1)S(1)}, u32[]{:S(2)}, u32[]{:S(2)}) collective-permute-start(bf16[512,256]{1,0:T(8,128)(2,1)S(1)} %bitcast.44), channel_id=1, source_target_pairs={{0,16},{16,32},{32,48},{48,64},{64,80},{80,96},{96,112},{112,128},... | collective-permute-start | bytes 786440 | tf_op jit(solution)/shard_map/ppermute | solution.py:289
  20.9 11.6 %collective-permute-start.1 = (bf16[128,256]{1,0:T(8,128)(2,1)S(1)}, bf16[128,256]{1,0:T(8,128)(2,1)S(1)}, u32[]{:S(2)}, u32[]{:S(2)}) collective-permute-start(bf16[128,256]{1,0:T(8,128)(2,1)S(1)} %reshape_squeeze.7), channel_id=1, source_target_pairs={{0,1},{1,2},{2,3},{3,4},{4,5},{5,6},{6,7},{7,8},{8,9},{9,10},{10,1... | collective-permute-start | bytes 196616 | tf_op jit(solution)/shard_map/ppermute | solution.py:289
  26.3 6.2 %collective-permute-start.2 = (bf16[32,256]{1,0:T(8,128)(2,1)S(1)}, bf16[32,256]{1,0:T(8,128)(2,1)S(1)}, u32[]{:S(2)}, u32[]{:S(2)}) collective-permute-start(bf16[32,256]{1,0:T(8,128)(2,1)S(1)} %bitcast.45), channel_id=1, source_target_pairs={{0,17},{1,18},{2,19},{3,20},{4,21},{5,22},{6,23},{7,24},{8,25},{9,... | collective-permute-start | bytes 49160 | tf_op jit(solution)/shard_map/ppermute | solution.py:306
  32.5 1.2 copy-start
  33.8 0.9 copy-start.3
  37.4 6.6 %collective-permute-start.3 = (bf16[64,64]{1,0:T(8,128)(2,1)S(1)}, bf16[64,64]{1,0:T(8,128)(2,1)S(1)}, u32[]{:S(2)}, u32[]{:S(2)}) collective-permute-start(bf16[64,64]{1,0:T(8,128)(2,1)S(1)} %get-tuple-element.20), channel_id=1, source_target_pairs={{0,1},{1,2},{2,3},{3,4},{4,5},{5,6},{6,7},{7,8},{8,9},{9,10},{10,1... | collective-permute-start | bytes 24584 | tf_op jit(solution)/shard_map/ppermute | solution.py:289
  42.7 5.7 %collective-permute-start.4 = (bf16[64,64]{1,0:T(8,128)(2,1)S(1)}, bf16[64,64]{1,0:T(8,128)(2,1)S(1)}, u32[]{:S(2)}, u32[]{:S(2)}) collective-permute-start(bf16[64,64]{1,0:T(8,128)(2,1)S(1)} %get-tuple-element.22), channel_id=1, source_target_pairs={{1,0},{2,1},{3,2},{4,3},{5,4},{6,5},{7,6},{8,7},{9,8},{10,9},{11,1... | collective-permute-start | bytes 24584 | tf_op jit(solution)/shard_map/ppermute | solution.py:289
  48.4 6.8 %collective-permute-start.5 = (bf16[64,384]{1,0:T(8,128)(2,1)S(1)}, bf16[64,384]{1,0:T(8,128)(2,1)S(1)}, u32[]{:S(2)}, u32[]{:S(2)}) collective-permute-start(bf16[64,384]{1,0:T(8,128)(2,1)S(1)} %pad_maximum_fusion.1.own_ref), channel_id=1, source_target_pairs={{0,16},{16,32},{32,48},{48,64},{64,80},{80,96},{96,112},{112,128},... | collective-permute-start | bytes 147464 | tf_op jit(solution)/shard_map/ppermute | solution.py:289
  53.3 5.4 %collective-permute-start.6 = (bf16[64,384]{1,0:T(8,128)(2,1)S(1)}, bf16[64,384]{1,0:T(8,128)(2,1)S(1)}, u32[]{:S(2)}, u32[]{:S(2)}) collective-permute-start(bf16[64,384]{1,0:T(8,128)(2,1)S(1)} %pad_maximum_fusion.1.own_ref), channel_id=1, source_target_pairs={{16,0},{32,16},{48,32},{64,48},{80,64},{96,80},{112,96},{128,112},... | collective-permute-start | bytes 147464 | tf_op jit(solution)/shard_map/ppermute | solution.py:289
  59.4 7.1 %collective-permute-start.7 = (bf16[128,64]{1,0:T(8,128)(2,1)S(1)}, bf16[128,64]{1,0:T(8,128)(2,1)S(1)}, u32[]{:S(2)}, u32[]{:S(2)}) collective-permute-start(bf16[128,64]{1,0:T(8,128)(2,1)S(1)} %get-tuple-element.23), channel_id=1, source_target_pairs={{0,1},{1,2},{2,3},{3,4},{4,5},{5,6},{6,7},{7,8},{8,9},{9,10},{10,1... | collective-permute-start | bytes 49160 | tf_op jit(solution)/shard_map/ppermute | solution.py:289
  65.1 6.2 %collective-permute-start.8 = (bf16[128,64]{1,0:T(8,128)(2,1)S(1)}, bf16[128,64]{1,0:T(8,128)(2,1)S(1)}, u32[]{:S(2)}, u32[]{:S(2)}) collective-permute-start(bf16[128,64]{1,0:T(8,128)(2,1)S(1)} %get-tuple-element.25), channel_id=1, source_target_pairs={{1,0},{2,1},{3,2},{4,3},{5,4},{6,5},{7,6},{8,7},{9,8},{10,9},{11,1... | collective-permute-start | bytes 49160 | tf_op jit(solution)/shard_map/ppermute | solution.py:289
  71.5 6.3 %collective-permute-start.10 = (bf16[128,384]{1,0:T(8,128)(2,1)S(1)}, bf16[128,384]{1,0:T(8,128)(2,1)S(1)}, u32[]{:S(2)}, u32[]{:S(2)}) collective-permute-start(bf16[128,384]{1,0:T(8,128)(2,1)S(1)} %pad_maximum_fusion.own_ref), channel_id=1, source_target_pairs={{16,0},{32,16},{48,32},{64,48},{80,64},{96,80},{112,96},{128,112},... | collective-permute-start | bytes 294920 | tf_op jit(solution)/shard_map/ppermute | solution.py:289
  73.4 5.3 %collective-permute-start.9 = (bf16[128,384]{1,0:T(8,128)(2,1)S(1)}, bf16[128,384]{1,0:T(8,128)(2,1)S(1)}, u32[]{:S(2)}, u32[]{:S(2)}) collective-permute-start(bf16[128,384]{1,0:T(8,128)(2,1)S(1)} %pad_maximum_fusion.own_ref), channel_id=1, source_target_pairs={{0,16},{16,32},{32,48},{48,64},{64,80},{80,96},{96,112},{112,128},... | collective-permute-start | bytes 294920 | tf_op jit(solution)/shard_map/ppermute | solution.py:289
